TPU v7x, 256 devices: a whole 4x4x8 slice. The times are simulated.
256 devices in a mesh: section: 8 (over z), dom: 16 (over y, x), ens: 2 (over core).
Axes of the slice: x: 4, y: 4, z: 8, core: 2. Of those that a mesh axis runs over, the one named last changes fastest.
Arguments:
- members: bfloat16 [16, 2048, 512], P(('section', 'ens'), 'dom'), may hold values from -6 to 6
- layer_mats: bfloat16 [8, 6, 512, 512], P('section'), may hold values from -0.25 to 0.25
- biases: float32 [8, 2, 512], P('section'), may hold values from -3 to 3
- norm_gains: float32 [8, 2, 512], P('section'), may hold values from 0.25 to 1.75
- edge_blocks: int32 [16, 6], P('dom'), may hold values from 0 to 2
- edge_shift: int32 [16, 6], P('dom'), may hold values from 0 to 127
Outputs:
- final_state: bfloat16 [16, 2048, 512], P(('section', 'ens'), 'dom')
- ens_mean: float32 [2048, 512], P('dom')
Inputs may be any that keep to these rules, and one draw needn't show every extreme that they name: `edge_blocks`: a frame of 1 block of the previous part (wrapping around), the part's own 1 block, then 1 block of the next part.
All inputs are finite; a program needn't handle non-finite values.
Results may differ from a plain program's by a relative error of at most 0.022.
Values may be sent and summed in bfloat16 or wider, within the bound.
A program may use at most 64 MiB of HBM per device.

v0:
```python
import jax
import jax.numpy as jnp
from jax import lax
from jax.sharding import PartitionSpec as P

BLK = 128
HB = 1


EPSILON = 1e-05


def with_halo(x, sides, width):
    for axis, dim in sides:
        devices, length = (lax.axis_size(axis), x.shape[dim])
        up = [(i, (i + 1) % devices) for i in range(devices)]
        down = [(j, i) for i, j in up]
        last = lax.slice_in_dim(x, length - width, length, axis=dim)
        first = lax.slice_in_dim(x, 0, width, axis=dim)
        before = lax.ppermute(last, axis, up)
        after = lax.ppermute(first, axis, down)
        x = jnp.concatenate([before, x, after], axis=dim)
    return x


def from_behind(x, axis, by):
    devices = lax.axis_size(axis)
    return lax.ppermute(x, axis, [(i, (i + by) % devices) for i in range(devices)])


def layer_norm(values):
    average = jnp.mean(values, axis=-1, keepdims=True)
    centred = values - average
    spread = jnp.mean(centred * centred, axis=-1, keepdims=True)
    return centred * lax.rsqrt(spread + EPSILON)


def project(values, weight):
    return jnp.einsum("mnd,de->mne", values, weight, preferred_element_type=jnp.float32)


def fetch_rim(state, send_weight):
    extended = with_halo(state, (("dom", 1),), HB * BLK)
    return project(extended, send_weight).astype(jnp.bfloat16)


def update_nodes(state, sender_terms, sender_rows, matrices, bias_pair, gain_pair):
    batch_size, node_count, width_d = state.shape
    slot_count = sender_rows.shape[1]
    receiver_terms = project(state, matrices[1]) + bias_pair[0]
    picked = jnp.take(sender_terms, sender_rows.reshape(-1), axis=1).reshape(
        batch_size, node_count, slot_count, width_d
    )
    pre_act = picked.astype(jnp.float32) + receiver_terms[:, :, None, :]
    hidden = jax.nn.silu(pre_act).astype(jnp.bfloat16)
    edge_out = jnp.einsum("mnkd,de->mnke", hidden, matrices[2], preferred_element_type=jnp.float32)
    messages = jnp.sum(layer_norm(edge_out) * gain_pair[0], axis=2).astype(jnp.bfloat16)
    node_pre = project(state, matrices[3]) + project(messages, matrices[4]) + bias_pair[1]
    node_hidden = jax.nn.silu(node_pre).astype(jnp.bfloat16)
    node_out = project(node_hidden, matrices[5])
    return (state.astype(jnp.float32) + layer_norm(node_out) * gain_pair[1]).astype(jnp.bfloat16)


def on_device(members, layer_mats, biases, norm_gains, edge_blocks, edge_shift):
    blocks = edge_blocks.shape[0]
    block_rows = jnp.repeat(edge_blocks, BLK, axis=0)
    row_offsets = jnp.repeat(edge_shift, BLK, axis=0)
    positions = (jnp.arange(blocks * BLK, dtype=jnp.int32) % BLK)[:, None]
    sender_rows = block_rows * BLK + (positions + row_offsets) % BLK
    sections = lax.axis_size("section")
    section_index = lax.axis_index("section")
    matrices = layer_mats[0]
    bias_pair = biases[0]
    gain_pair = norm_gains[0]

    def advance(moment, state):
        anchor = (section_index - moment) % sections
        entry_tick = (sections - anchor) % sections
        active = jnp.logical_and(moment >= entry_tick, moment - entry_tick < sections)
        sender_terms = fetch_rim(state, matrices[0])
        state = lax.cond(
            active,
            lambda: update_nodes(state, sender_terms, sender_rows, matrices, bias_pair, gain_pair),
            lambda: state,
        )
        return from_behind(state, "section", 1)

    final_state = lax.fori_loop(0, 2 * sections, advance, members)
    member_count = final_state.shape[0] * sections * lax.axis_size("ens")
    member_total = lax.psum(
        jnp.sum(final_state.astype(jnp.float32), axis=0).astype(jnp.bfloat16), ("section", "ens")
    ).astype(jnp.float32)
    return (final_state, member_total / member_count)


def solution(mesh):
    placed = (
        P(("section", "ens"), "dom", None),
        P("section", None, None, None),
        P("section", None, None),
        P("section", None, None),
        P("dom", None),
        P("dom", None),
    )
    return jax.shard_map(
        on_device,
        mesh=mesh,
        in_specs=placed,
        out_specs=(P(("section", "ens"), "dom", None), P("dom", None)),
        check_vma=False,
    )
```

profile of v0, /device:TPU:1, one launch (start us, length us, event | category | flops | bytes accessed | tf_op | source)
XLA Modules:
  0.0 643.1 jit_solution(16240363588109194003)
XLA Ops:
  10.5 489.8 %while.19 = (s32[]{:T(128)}, bf16[1,128,512]{2,1,0:T(8,128)(2,1)}, s32[]{:T(128)}, bf16[6,512,512]{2,1,0:T(8,128)(2,1)}, f32[2,512]{1,0:T(2,128)}, /*index=5*/f3...) while((s32[]{:T(128)}, bf16[1,128,512]{2,1,0:T(8,128)(2,1)}, ...), condition=%wide.region_8.9_spmd.clone, body=%wide.region_0.8_spmd.clone.sunk | while | flops 881215872 | bytes 43935020 | solution.py:88
  10.5 5.8 collective-permute-start
  18.8 4.9 collective-permute-done.1
  25.2 17.0 %conditional.3 = (bf16[1,128,512]{2,1,0:T(8,128)(2,1)}) conditional(s32[]{:T(128)} %convert_element_type.119, bf16[1,128,512]{2,1,0:T(8,128)(2,1)} %get-tuple-element.368, (bf16[1,128,512]{2,1,0:T(8,128)(2,1)}, bf16[6,512,512]{2,1,0:T(8,128)(2,1)}, s32[6]{0:T(128)}, bf16[384,512]{1,0:T(8,128)(2,1)S(1)}, f32[2,512]{1,0:T(2,128)S(1)}, ...), branch_computations={%region_1.1_spmd, %region_2.7_spmd.clone} | conditional | flops 678507648 | bytes 40749172 | solution.py:81
  29.6 2.7 gather_fusion
  36.9 1.8 fusion.10
  42.1 5.2 collective-permute-done.2
  52.1 3.9 collective-permute-done.1
  57.5 17.0 %conditional.3 = (bf16[1,128,512]{2,1,0:T(8,128)(2,1)}) conditional(s32[]{:T(128)} %convert_element_type.119, bf16[1,128,512]{2,1,0:T(8,128)(2,1)} %get-tuple-element.368, (bf16[1,128,512]{2,1,0:T(8,128)(2,1)}, bf16[6,512,512]{2,1,0:T(8,128)(2,1)}, s32[6]{0:T(128)}, bf16[384,512]{1,0:T(8,128)(2,1)S(1)}, f32[2,512]{1,0:T(2,128)S(1)}, ...), branch_computations={%region_1.1_spmd, %region_2.7_spmd.clone} | conditional | flops 678507648 | bytes 40749172 | solution.py:81
  61.9 2.7 gather_fusion
  69.2 1.8 fusion.10
  74.4 5.2 collective-permute-done.2
  82.5 2.0 collective-permute-done
  84.5 3.1 collective-permute-done.1
  89.2 17.0 %conditional.3 = (bf16[1,128,512]{2,1,0:T(8,128)(2,1)}) conditional(s32[]{:T(128)} %convert_element_type.119, bf16[1,128,512]{2,1,0:T(8,128)(2,1)} %get-tuple-element.368, (bf16[1,128,512]{2,1,0:T(8,128)(2,1)}, bf16[6,512,512]{2,1,0:T(8,128)(2,1)}, s32[6]{0:T(128)}, bf16[384,512]{1,0:T(8,128)(2,1)S(1)}, f32[2,512]{1,0:T(2,128)S(1)}, ...), branch_computations={%region_1.1_spmd, %region_2.7_spmd.clone} | conditional | flops 678507648 | bytes 40749172 | solution.py:81
  93.7 2.7 gather_fusion
  100.9 1.8 fusion.10
  106.2 5.2 collective-permute-done.2
  116.1 3.3 collective-permute-done.1
  120.9 17.0 %conditional.3 = (bf16[1,128,512]{2,1,0:T(8,128)(2,1)}) conditional(s32[]{:T(128)} %convert_element_type.119, bf16[1,128,512]{2,1,0:T(8,128)(2,1)} %get-tuple-element.368, (bf16[1,128,512]{2,1,0:T(8,128)(2,1)}, bf16[6,512,512]{2,1,0:T(8,128)(2,1)}, s32[6]{0:T(128)}, bf16[384,512]{1,0:T(8,128)(2,1)S(1)}, f32[2,512]{1,0:T(2,128)S(1)}, ...), branch_computations={%region_1.1_spmd, %region_2.7_spmd.clone} | conditional | flops 678507648 | bytes 40749172 | solution.py:81
  125.4 2.7 gather_fusion
  132.7 1.8 fusion.10
  137.9 5.2 collective-permute-done.2
  147.8 3.3 collective-permute-done.1
  152.7 17.0 %conditional.3 = (bf16[1,128,512]{2,1,0:T(8,128)(2,1)}) conditional(s32[]{:T(128)} %convert_element_type.119, bf16[1,128,512]{2,1,0:T(8,128)(2,1)} %get-tuple-element.368, (bf16[1,128,512]{2,1,0:T(8,128)(2,1)}, bf16[6,512,512]{2,1,0:T(8,128)(2,1)}, s32[6]{0:T(128)}, bf16[384,512]{1,0:T(8,128)(2,1)S(1)}, f32[2,512]{1,0:T(2,128)S(1)}, ...), branch_computations={%region_1.1_spmd, %region_2.7_spmd.clone} | conditional | flops 678507648 | bytes 40749172 | solution.py:81
  157.1 2.7 gather_fusion
  164.4 1.8 fusion.10
  169.6 5.2 collective-permute-done.2
  179.6 3.3 collective-permute-done.1
  184.4 17.0 %conditional.3 = (bf16[1,128,512]{2,1,0:T(8,128)(2,1)}) conditional(s32[]{:T(128)} %convert_element_type.119, bf16[1,128,512]{2,1,0:T(8,128)(2,1)} %get-tuple-element.368, (bf16[1,128,512]{2,1,0:T(8,128)(2,1)}, bf16[6,512,512]{2,1,0:T(8,128)(2,1)}, s32[6]{0:T(128)}, bf16[384,512]{1,0:T(8,128)(2,1)S(1)}, f32[2,512]{1,0:T(2,128)S(1)}, ...), branch_computations={%region_1.1_spmd, %region_2.7_spmd.clone} | conditional | flops 678507648 | bytes 40749172 | solution.py:81
  188.9 2.7 gather_fusion
  196.2 1.8 fusion.10
  201.4 5.2 collective-permute-done.2
  211.3 3.3 collective-permute-done.1
  216.2 17.0 %conditional.3 = (bf16[1,128,512]{2,1,0:T(8,128)(2,1)}) conditional(s32[]{:T(128)} %convert_element_type.119, bf16[1,128,512]{2,1,0:T(8,128)(2,1)} %get-tuple-element.368, (bf16[1,128,512]{2,1,0:T(8,128)(2,1)}, bf16[6,512,512]{2,1,0:T(8,128)(2,1)}, s32[6]{0:T(128)}, bf16[384,512]{1,0:T(8,128)(2,1)S(1)}, f32[2,512]{1,0:T(2,128)S(1)}, ...), branch_computations={%region_1.1_spmd, %region_2.7_spmd.clone} | conditional | flops 678507648 | bytes 40749172 | solution.py:81
  220.6 2.7 gather_fusion
  227.9 1.8 fusion.10
  233.1 5.2 collective-permute-done.2
  243.0 3.3 collective-permute-done.1
  247.9 17.0 %conditional.3 = (bf16[1,128,512]{2,1,0:T(8,128)(2,1)}) conditional(s32[]{:T(128)} %convert_element_type.119, bf16[1,128,512]{2,1,0:T(8,128)(2,1)} %get-tuple-element.368, (bf16[1,128,512]{2,1,0:T(8,128)(2,1)}, bf16[6,512,512]{2,1,0:T(8,128)(2,1)}, s32[6]{0:T(128)}, bf16[384,512]{1,0:T(8,128)(2,1)S(1)}, f32[2,512]{1,0:T(2,128)S(1)}, ...), branch_computations={%region_1.1_spmd, %region_2.7_spmd.clone} | conditional | flops 678507648 | bytes 40749172 | solution.py:81
  252.4 2.7 gather_fusion
  259.6 1.8 fusion.10
  264.9 5.2 collective-permute-done.2
  274.8 3.3 collective-permute-done.1
  279.6 15.7 %collective-permute-start.2 = (bf16[1,128,512]{2,1,0:T(8,128)(2,1)}, bf16[1,128,512]{2,1,0:T(8,128)(2,1)S(1)}, u32[]{:S(2)}, u32[]{:S(2)}) collective-permute-start(bf16[1,128,512]{2,1,0:T(8,128)(2,1)} %get-tuple-element.393), channel_id=1, source_target_pairs={{0,32},{32,64},{64,96},{96,128},{128,160},{160,192},{192,224},{224... | collective-permute-start | bytes 393224 | tf_op jit(solution)/shard_map/while/body/eval_jaxpr/ppermute | solution.py:28
  295.4 3.5 collective-permute-done.2
  303.5 3.3 collective-permute-done.1
  309.0 20.3 %collective-permute-done.2 = bf16[1,128,512]{2,1,0:T(8,128)(2,1)S(1)} collective-permute-done((bf16[1,128,512]{2,1,0:T(8,128)(2,1)}, bf16[1,128,512]{2,1,0:T(8,128)(2,1)S(1)}, u32[]{:S(2)}, u32[]{:S(2)}) %collective-permute-start.2) | collective-permute-done | bytes 131104 | tf_op jit(solution)/shard_map/while/body/eval_jaxpr/ppermute | solution.py:28
  334.1 3.3 collective-permute-done.1
  339.0 21.2 %collective-permute-done.2 = bf16[1,128,512]{2,1,0:T(8,128)(2,1)S(1)} collective-permute-done((bf16[1,128,512]{2,1,0:T(8,128)(2,1)}, bf16[1,128,512]{2,1,0:T(8,128)(2,1)S(1)}, u32[]{:S(2)}, u32[]{:S(2)}) %collective-permute-start.2) | collective-permute-done | bytes 131104 | tf_op jit(solution)/shard_map/while/body/eval_jaxpr/ppermute | solution.py:28
  364.9 3.3 collective-permute-done.1
  369.9 20.9 %collective-permute-done.2 = bf16[1,128,512]{2,1,0:T(8,128)(2,1)S(1)} collective-permute-done((bf16[1,128,512]{2,1,0:T(8,128)(2,1)}, bf16[1,128,512]{2,1,0:T(8,128)(2,1)S(1)}, u32[]{:S(2)}, u32[]{:S(2)}) %collective-permute-start.2) | collective-permute-done | bytes 131104 | tf_op jit(solution)/shard_map/while/body/eval_jaxpr/ppermute | solution.py:28
  395.4 3.3 collective-permute-done.1
  400.4 21.2 %collective-permute-done.2 = bf16[1,128,512]{2,1,0:T(8,128)(2,1)S(1)} collective-permute-done((bf16[1,128,512]{2,1,0:T(8,128)(2,1)}, bf16[1,128,512]{2,1,0:T(8,128)(2,1)S(1)}, u32[]{:S(2)}, u32[]{:S(2)}) %collective-permute-start.2) | collective-permute-done | bytes 131104 | tf_op jit(solution)/shard_map/while/body/eval_jaxpr/ppermute | solution.py:28
  424.4 2.1 collective-permute-done
  426.5 3.0 collective-permute-done.1
  431.2 20.9 %collective-permute-done.2 = bf16[1,128,512]{2,1,0:T(8,128)(2,1)S(1)} collective-permute-done((bf16[1,128,512]{2,1,0:T(8,128)(2,1)}, bf16[1,128,512]{2,1,0:T(8,128)(2,1)S(1)}, u32[]{:S(2)}, u32[]{:S(2)}) %collective-permute-start.2) | collective-permute-done | bytes 131104 | tf_op jit(solution)/shard_map/while/body/eval_jaxpr/ppermute | solution.py:28
  454.9 2.5 collective-permute-done
  457.5 3.3 collective-permute-done.1
  462.4 22.4 %collective-permute-done.2 = bf16[1,128,512]{2,1,0:T(8,128)(2,1)S(1)} collective-permute-done((bf16[1,128,512]{2,1,0:T(8,128)(2,1)}, bf16[1,128,512]{2,1,0:T(8,128)(2,1)S(1)}, u32[]{:S(2)}, u32[]{:S(2)}) %collective-permute-start.2) | collective-permute-done | bytes 131104 | tf_op jit(solution)/shard_map/while/body/eval_jaxpr/ppermute | solution.py:28
  487.7 2.1 collective-permute-done
  489.8 3.0 collective-permute-done.1
  494.4 5.2 collective-permute-done.2
  500.3 134.3 %all-reduce.2.cloned.1.call-done = bf16[128,512]{1,0:T(8,128)(2,1)} async-done(((bf16[128,512]{1,0:T(8,128)(2,1)}), bf16[128,512]{1,0:T(8,128)(2,1)}) %all-reduce.2.cloned.1.call-update) | async-done | bytes 131088 | tf_op jit(solution)/shard_map/psum | solution.py:90
  (424 shorter events, 194.3 us)
Async XLA Ops:
  7.2 627.4 %all-reduce.2.cloned.1.call-start = ((), (), s32[]{:S(2)}) async-start(), calls=%async_computation | async-start | bytes 262144 | tf_op jit(solution)/shard_map/psum | solution.py:90
  10.5 14.6 %copy-start.2 = (f32[2,512]{1,0:T(2,128)S(1)}, f32[2,512]{1,0:T(2,128)}, u32[]{:S(2)}) copy-start(f32[2,512]{1,0:T(2,128)} %get-tuple-element.384) | copy-start | bytes 12292 | tf_op jit(solution)/shard_map/while
  10.5 14.6 %copy-start.3 = (f32[2,512]{1,0:T(2,128)S(1)}, f32[2,512]{1,0:T(2,128)}, u32[]{:S(2)}) copy-start(f32[2,512]{1,0:T(2,128)} %get-tuple-element.385) | copy-start | bytes 12292 | tf_op jit(solution)/shard_map/while
  10.5 8.2 %collective-permute-start = (bf16[1,128,512]{2,1,0:T(8,128)(2,1)}, bf16[1,128,512]{2,1,0:T(8,128)(2,1)S(1)}, u32[]{:S(2)}, u32[]{:S(2)}) collective-permute-start(bf16[1,128,512]{2,1,0:T(8,128)(2,1)} %get-tuple-element.368), channel_id=1, source_target_pairs={{2,0},{4,2},{6,4},{8,6},{10,8},{12,10},{14,12},{16,14},{18,16},{20... | collective-permute-start | bytes 393224 | tf_op jit(solution)/shard_map/while/body/eval_jaxpr/ppermute | solution.py:21
  16.3 7.3 %collective-permute-start.1 = (bf16[1,128,512]{2,1,0:T(8,128)(2,1)}, bf16[1,128,512]{2,1,0:T(8,128)(2,1)S(1)}, u32[]{:S(2)}, u32[]{:S(2)}) collective-permute-start(bf16[1,128,512]{2,1,0:T(8,128)(2,1)} %get-tuple-element.368), channel_id=1, source_target_pairs={{0,2},{2,4},{4,6},{6,8},{8,10},{10,12},{12,14},{14,16},{16,18},{18... | collective-permute-start | bytes 393224 | tf_op jit(solution)/shard_map/while/body/eval_jaxpr/ppermute | solution.py:20
  42.1 5.2 collective-permute-start.2
  48.0 9.4 %copy-start.2 = (f32[2,512]{1,0:T(2,128)S(1)}, f32[2,512]{1,0:T(2,128)}, u32[]{:S(2)}) copy-start(f32[2,512]{1,0:T(2,128)} %get-tuple-element.384) | copy-start | bytes 12292 | tf_op jit(solution)/shard_map/while
  48.0 9.4 %copy-start.3 = (f32[2,512]{1,0:T(2,128)S(1)}, f32[2,512]{1,0:T(2,128)}, u32[]{:S(2)}) copy-start(f32[2,512]{1,0:T(2,128)} %get-tuple-element.385) | copy-start | bytes 12292 | tf_op jit(solution)/shard_map/while
  48.0 4.0 collective-permute-start
  48.6 7.3 %collective-permute-start.1 = (bf16[1,128,512]{2,1,0:T(8,128)(2,1)}, bf16[1,128,512]{2,1,0:T(8,128)(2,1)S(1)}, u32[]{:S(2)}, u32[]{:S(2)}) collective-permute-start(bf16[1,128,512]{2,1,0:T(8,128)(2,1)} %get-tuple-element.368), channel_id=1, source_target_pairs={{0,2},{2,4},{4,6},{6,8},{8,10},{10,12},{12,14},{14,16},{16,18},{18... | collective-permute-start | bytes 393224 | tf_op jit(solution)/shard_map/while/body/eval_jaxpr/ppermute | solution.py:20
  74.4 5.2 collective-permute-start.2
  80.3 8.9 %copy-start.3 = (f32[2,512]{1,0:T(2,128)S(1)}, f32[2,512]{1,0:T(2,128)}, u32[]{:S(2)}) copy-start(f32[2,512]{1,0:T(2,128)} %get-tuple-element.385) | copy-start | bytes 12292 | tf_op jit(solution)/shard_map/while
  80.3 4.2 collective-permute-start
  80.3 7.3 %collective-permute-start.1 = (bf16[1,128,512]{2,1,0:T(8,128)(2,1)}, bf16[1,128,512]{2,1,0:T(8,128)(2,1)S(1)}, u32[]{:S(2)}, u32[]{:S(2)}) collective-permute-start(bf16[1,128,512]{2,1,0:T(8,128)(2,1)} %get-tuple-element.368), channel_id=1, source_target_pairs={{0,2},{2,4},{4,6},{6,8},{8,10},{10,12},{12,14},{14,16},{16,18},{18... | collective-permute-start | bytes 393224 | tf_op jit(solution)/shard_map/while/body/eval_jaxpr/ppermute | solution.py:20
  106.2 5.2 collective-permute-start.2
  112.1 4.0 collective-permute-start
  112.1 7.3 %collective-permute-start.1 = (bf16[1,128,512]{2,1,0:T(8,128)(2,1)}, bf16[1,128,512]{2,1,0:T(8,128)(2,1)S(1)}, u32[]{:S(2)}, u32[]{:S(2)}) collective-permute-start(bf16[1,128,512]{2,1,0:T(8,128)(2,1)} %get-tuple-element.368), channel_id=1, source_target_pairs={{0,2},{2,4},{4,6},{6,8},{8,10},{10,12},{12,14},{14,16},{16,18},{18... | collective-permute-start | bytes 393224 | tf_op jit(solution)/shard_map/while/body/eval_jaxpr/ppermute | solution.py:20
  137.9 5.2 collective-permute-start.2
  143.8 8.9 %copy-start.2 = (f32[2,512]{1,0:T(2,128)S(1)}, f32[2,512]{1,0:T(2,128)}, u32[]{:S(2)}) copy-start(f32[2,512]{1,0:T(2,128)} %get-tuple-element.384) | copy-start | bytes 12292 | tf_op jit(solution)/shard_map/while
  143.8 8.9 %copy-start.3 = (f32[2,512]{1,0:T(2,128)S(1)}, f32[2,512]{1,0:T(2,128)}, u32[]{:S(2)}) copy-start(f32[2,512]{1,0:T(2,128)} %get-tuple-element.385) | copy-start | bytes 12292 | tf_op jit(solution)/shard_map/while
  143.8 4.0 collective-permute-start
  143.8 7.3 %collective-permute-start.1 = (bf16[1,128,512]{2,1,0:T(8,128)(2,1)}, bf16[1,128,512]{2,1,0:T(8,128)(2,1)S(1)}, u32[]{:S(2)}, u32[]{:S(2)}) collective-permute-start(bf16[1,128,512]{2,1,0:T(8,128)(2,1)} %get-tuple-element.368), channel_id=1, source_target_pairs={{0,2},{2,4},{4,6},{6,8},{8,10},{10,12},{12,14},{14,16},{16,18},{18... | collective-permute-start | bytes 393224 | tf_op jit(solution)/shard_map/while/body/eval_jaxpr/ppermute | solution.py:20
  169.6 5.2 collective-permute-start.2
  175.5 8.9 %copy-start.3 = (f32[2,512]{1,0:T(2,128)S(1)}, f32[2,512]{1,0:T(2,128)}, u32[]{:S(2)}) copy-start(f32[2,512]{1,0:T(2,128)} %get-tuple-element.385) | copy-start | bytes 12292 | tf_op jit(solution)/shard_map/while
  175.5 4.0 collective-permute-start
  175.5 7.3 %collective-permute-start.1 = (bf16[1,128,512]{2,1,0:T(8,128)(2,1)}, bf16[1,128,512]{2,1,0:T(8,128)(2,1)S(1)}, u32[]{:S(2)}, u32[]{:S(2)}) collective-permute-start(bf16[1,128,512]{2,1,0:T(8,128)(2,1)} %get-tuple-element.368), channel_id=1, source_target_pairs={{0,2},{2,4},{4,6},{6,8},{8,10},{10,12},{12,14},{14,16},{16,18},{18... | collective-permute-start | bytes 393224 | tf_op jit(solution)/shard_map/while/body/eval_jaxpr/ppermute | solution.py:20
  201.4 5.2 collective-permute-start.2
  207.3 4.0 collective-permute-start
  207.3 7.3 %collective-permute-start.1 = (bf16[1,128,512]{2,1,0:T(8,128)(2,1)}, bf16[1,128,512]{2,1,0:T(8,128)(2,1)S(1)}, u32[]{:S(2)}, u32[]{:S(2)}) collective-permute-start(bf16[1,128,512]{2,1,0:T(8,128)(2,1)} %get-tuple-element.368), channel_id=1, source_target_pairs={{0,2},{2,4},{4,6},{6,8},{8,10},{10,12},{12,14},{14,16},{16,18},{18... | collective-permute-start | bytes 393224 | tf_op jit(solution)/shard_map/while/body/eval_jaxpr/ppermute | solution.py:20
  233.1 5.2 collective-permute-start.2
  239.0 8.9 %copy-start.2 = (f32[2,512]{1,0:T(2,128)S(1)}, f32[2,512]{1,0:T(2,128)}, u32[]{:S(2)}) copy-start(f32[2,512]{1,0:T(2,128)} %get-tuple-element.384) | copy-start | bytes 12292 | tf_op jit(solution)/shard_map/while
  239.0 8.9 %copy-start.3 = (f32[2,512]{1,0:T(2,128)S(1)}, f32[2,512]{1,0:T(2,128)}, u32[]{:S(2)}) copy-start(f32[2,512]{1,0:T(2,128)} %get-tuple-element.385) | copy-start | bytes 12292 | tf_op jit(solution)/shard_map/while
  239.0 4.0 collective-permute-start
  239.0 7.3 %collective-permute-start.1 = (bf16[1,128,512]{2,1,0:T(8,128)(2,1)}, bf16[1,128,512]{2,1,0:T(8,128)(2,1)S(1)}, u32[]{:S(2)}, u32[]{:S(2)}) collective-permute-start(bf16[1,128,512]{2,1,0:T(8,128)(2,1)} %get-tuple-element.368), channel_id=1, source_target_pairs={{0,2},{2,4},{4,6},{6,8},{8,10},{10,12},{12,14},{14,16},{16,18},{18... | collective-permute-start | bytes 393224 | tf_op jit(solution)/shard_map/while/body/eval_jaxpr/ppermute | solution.py:20
  264.9 5.2 collective-permute-start.2
  270.8 8.9 %copy-start.3 = (f32[2,512]{1,0:T(2,128)S(1)}, f32[2,512]{1,0:T(2,128)}, u32[]{:S(2)}) copy-start(f32[2,512]{1,0:T(2,128)} %get-tuple-element.385) | copy-start | bytes 12292 | tf_op jit(solution)/shard_map/while
  270.8 4.0 collective-permute-start
  270.8 7.3 %collective-permute-start.1 = (bf16[1,128,512]{2,1,0:T(8,128)(2,1)}, bf16[1,128,512]{2,1,0:T(8,128)(2,1)S(1)}, u32[]{:S(2)}, u32[]{:S(2)}) collective-permute-start(bf16[1,128,512]{2,1,0:T(8,128)(2,1)} %get-tuple-element.368), channel_id=1, source_target_pairs={{0,2},{2,4},{4,6},{6,8},{8,10},{10,12},{12,14},{14,16},{16,18},{18... | collective-permute-start | bytes 393224 | tf_op jit(solution)/shard_map/while/body/eval_jaxpr/ppermute | solution.py:20
  279.6 19.2 %collective-permute-start.2 = (bf16[1,128,512]{2,1,0:T(8,128)(2,1)}, bf16[1,128,512]{2,1,0:T(8,128)(2,1)S(1)}, u32[]{:S(2)}, u32[]{:S(2)}) collective-permute-start(bf16[1,128,512]{2,1,0:T(8,128)(2,1)} %get-tuple-element.393), channel_id=1, source_target_pairs={{0,32},{32,64},{64,96},{96,128},{128,160},{160,192},{192,224},{224... | collective-permute-start | bytes 393224 | tf_op jit(solution)/shard_map/while/body/eval_jaxpr/ppermute | solution.py:28
  299.5 4.0 collective-permute-start
  299.5 7.3 %collective-permute-start.1 = (bf16[1,128,512]{2,1,0:T(8,128)(2,1)}, bf16[1,128,512]{2,1,0:T(8,128)(2,1)S(1)}, u32[]{:S(2)}, u32[]{:S(2)}) collective-permute-start(bf16[1,128,512]{2,1,0:T(8,128)(2,1)} %get-tuple-element.368), channel_id=1, source_target_pairs={{0,2},{2,4},{4,6},{6,8},{8,10},{10,12},{12,14},{14,16},{16,18},{18... | collective-permute-start | bytes 393224 | tf_op jit(solution)/shard_map/while/body/eval_jaxpr/ppermute | solution.py:20
  308.4 21.0 %collective-permute-start.2 = (bf16[1,128,512]{2,1,0:T(8,128)(2,1)}, bf16[1,128,512]{2,1,0:T(8,128)(2,1)S(1)}, u32[]{:S(2)}, u32[]{:S(2)}) collective-permute-start(bf16[1,128,512]{2,1,0:T(8,128)(2,1)} %get-tuple-element.393), channel_id=1, source_target_pairs={{0,32},{32,64},{64,96},{96,128},{128,160},{160,192},{192,224},{224... | collective-permute-start | bytes 393224 | tf_op jit(solution)/shard_map/while/body/eval_jaxpr/ppermute | solution.py:28
  330.0 4.0 collective-permute-start
  330.1 7.3 %collective-permute-start.1 = (bf16[1,128,512]{2,1,0:T(8,128)(2,1)}, bf16[1,128,512]{2,1,0:T(8,128)(2,1)S(1)}, u32[]{:S(2)}, u32[]{:S(2)}) collective-permute-start(bf16[1,128,512]{2,1,0:T(8,128)(2,1)} %get-tuple-element.368), channel_id=1, source_target_pairs={{0,2},{2,4},{4,6},{6,8},{8,10},{10,12},{12,14},{14,16},{16,18},{18... | collective-permute-start | bytes 393224 | tf_op jit(solution)/shard_map/while/body/eval_jaxpr/ppermute | solution.py:20
  338.9 21.3 %collective-permute-start.2 = (bf16[1,128,512]{2,1,0:T(8,128)(2,1)}, bf16[1,128,512]{2,1,0:T(8,128)(2,1)S(1)}, u32[]{:S(2)}, u32[]{:S(2)}) collective-permute-start(bf16[1,128,512]{2,1,0:T(8,128)(2,1)} %get-tuple-element.393), channel_id=1, source_target_pairs={{0,32},{32,64},{64,96},{96,128},{128,160},{160,192},{192,224},{224... | collective-permute-start | bytes 393224 | tf_op jit(solution)/shard_map/while/body/eval_jaxpr/ppermute | solution.py:28
  360.9 8.9 %copy-start.2 = (f32[2,512]{1,0:T(2,128)S(1)}, f32[2,512]{1,0:T(2,128)}, u32[]{:S(2)}) copy-start(f32[2,512]{1,0:T(2,128)} %get-tuple-element.384) | copy-start | bytes 12292 | tf_op jit(solution)/shard_map/while
  360.9 8.9 %copy-start.3 = (f32[2,512]{1,0:T(2,128)S(1)}, f32[2,512]{1,0:T(2,128)}, u32[]{:S(2)}) copy-start(f32[2,512]{1,0:T(2,128)} %get-tuple-element.385) | copy-start | bytes 12292 | tf_op jit(solution)/shard_map/while
  360.9 4.0 collective-permute-start
  360.9 7.3 %collective-permute-start.1 = (bf16[1,128,512]{2,1,0:T(8,128)(2,1)}, bf16[1,128,512]{2,1,0:T(8,128)(2,1)S(1)}, u32[]{:S(2)}, u32[]{:S(2)}) collective-permute-start(bf16[1,128,512]{2,1,0:T(8,128)(2,1)} %get-tuple-element.368), channel_id=1, source_target_pairs={{0,2},{2,4},{4,6},{6,8},{8,10},{10,12},{12,14},{14,16},{16,18},{18... | collective-permute-start | bytes 393224 | tf_op jit(solution)/shard_map/while/body/eval_jaxpr/ppermute | solution.py:20
  369.8 21.0 %collective-permute-start.2 = (bf16[1,128,512]{2,1,0:T(8,128)(2,1)}, bf16[1,128,512]{2,1,0:T(8,128)(2,1)S(1)}, u32[]{:S(2)}, u32[]{:S(2)}) collective-permute-start(bf16[1,128,512]{2,1,0:T(8,128)(2,1)} %get-tuple-element.393), channel_id=1, source_target_pairs={{0,32},{32,64},{64,96},{96,128},{128,160},{160,192},{192,224},{224... | collective-permute-start | bytes 393224 | tf_op jit(solution)/shard_map/while/body/eval_jaxpr/ppermute | solution.py:28
  391.4 4.0 collective-permute-start
  391.4 7.3 %collective-permute-start.1 = (bf16[1,128,512]{2,1,0:T(8,128)(2,1)}, bf16[1,128,512]{2,1,0:T(8,128)(2,1)S(1)}, u32[]{:S(2)}, u32[]{:S(2)}) collective-permute-start(bf16[1,128,512]{2,1,0:T(8,128)(2,1)} %get-tuple-element.368), channel_id=1, source_target_pairs={{0,2},{2,4},{4,6},{6,8},{8,10},{10,12},{12,14},{14,16},{16,18},{18... | collective-permute-start | bytes 393224 | tf_op jit(solution)/shard_map/while/body/eval_jaxpr/ppermute | solution.py:20
  400.3 21.2 %collective-permute-start.2 = (bf16[1,128,512]{2,1,0:T(8,128)(2,1)}, bf16[1,128,512]{2,1,0:T(8,128)(2,1)S(1)}, u32[]{:S(2)}, u32[]{:S(2)}) collective-permute-start(bf16[1,128,512]{2,1,0:T(8,128)(2,1)} %get-tuple-element.393), channel_id=1, source_target_pairs={{0,32},{32,64},{64,96},{96,128},{128,160},{160,192},{192,224},{224... | collective-permute-start | bytes 393224 | tf_op jit(solution)/shard_map/while/body/eval_jaxpr/ppermute | solution.py:28
  422.2 4.3 collective-permute-start
  422.2 7.3 %collective-permute-start.1 = (bf16[1,128,512]{2,1,0:T(8,128)(2,1)}, bf16[1,128,512]{2,1,0:T(8,128)(2,1)S(1)}, u32[]{:S(2)}, u32[]{:S(2)}) collective-permute-start(bf16[1,128,512]{2,1,0:T(8,128)(2,1)} %get-tuple-element.368), channel_id=1, source_target_pairs={{0,2},{2,4},{4,6},{6,8},{8,10},{10,12},{12,14},{14,16},{16,18},{18... | collective-permute-start | bytes 393224 | tf_op jit(solution)/shard_map/while/body/eval_jaxpr/ppermute | solution.py:20
  431.1 21.0 %collective-permute-start.2 = (bf16[1,128,512]{2,1,0:T(8,128)(2,1)}, bf16[1,128,512]{2,1,0:T(8,128)(2,1)S(1)}, u32[]{:S(2)}, u32[]{:S(2)}) collective-permute-start(bf16[1,128,512]{2,1,0:T(8,128)(2,1)} %get-tuple-element.393), channel_id=1, source_target_pairs={{0,32},{32,64},{64,96},{96,128},{128,160},{160,192},{192,224},{224... | collective-permute-start | bytes 393224 | tf_op jit(solution)/shard_map/while/body/eval_jaxpr/ppermute | solution.py:28
  452.7 9.6 %copy-start.2 = (f32[2,512]{1,0:T(2,128)S(1)}, f32[2,512]{1,0:T(2,128)}, u32[]{:S(2)}) copy-start(f32[2,512]{1,0:T(2,128)} %get-tuple-element.384) | copy-start | bytes 12292 | tf_op jit(solution)/shard_map/while
  452.7 9.6 %copy-start.3 = (f32[2,512]{1,0:T(2,128)S(1)}, f32[2,512]{1,0:T(2,128)}, u32[]{:S(2)}) copy-start(f32[2,512]{1,0:T(2,128)} %get-tuple-element.385) | copy-start | bytes 12292 | tf_op jit(solution)/shard_map/while
  452.7 4.8 collective-permute-start
  452.7 8.1 %collective-permute-start.1 = (bf16[1,128,512]{2,1,0:T(8,128)(2,1)}, bf16[1,128,512]{2,1,0:T(8,128)(2,1)S(1)}, u32[]{:S(2)}, u32[]{:S(2)}) collective-permute-start(bf16[1,128,512]{2,1,0:T(8,128)(2,1)} %get-tuple-element.368), channel_id=1, source_target_pairs={{0,2},{2,4},{4,6},{6,8},{8,10},{10,12},{12,14},{14,16},{16,18},{18... | collective-permute-start | bytes 393224 | tf_op jit(solution)/shard_map/while/body/eval_jaxpr/ppermute | solution.py:20
  462.3 22.5 %collective-permute-start.2 = (bf16[1,128,512]{2,1,0:T(8,128)(2,1)}, bf16[1,128,512]{2,1,0:T(8,128)(2,1)S(1)}, u32[]{:S(2)}, u32[]{:S(2)}) collective-permute-start(bf16[1,128,512]{2,1,0:T(8,128)(2,1)} %get-tuple-element.393), channel_id=1, source_target_pairs={{0,32},{32,64},{64,96},{96,128},{128,160},{160,192},{192,224},{224... | collective-permute-start | bytes 393224 | tf_op jit(solution)/shard_map/while/body/eval_jaxpr/ppermute | solution.py:28
  485.4 4.3 collective-permute-start
  485.4 7.3 %collective-permute-start.1 = (bf16[1,128,512]{2,1,0:T(8,128)(2,1)}, bf16[1,128,512]{2,1,0:T(8,128)(2,1)S(1)}, u32[]{:S(2)}, u32[]{:S(2)}) collective-permute-start(bf16[1,128,512]{2,1,0:T(8,128)(2,1)} %get-tuple-element.368), channel_id=1, source_target_pairs={{0,2},{2,4},{4,6},{6,8},{8,10},{10,12},{12,14},{14,16},{16,18},{18... | collective-permute-start | bytes 393224 | tf_op jit(solution)/shard_map/while/body/eval_jaxpr/ppermute | solution.py:20
  494.3 5.3 collective-permute-start.2
  (41 other events, 215.8 us)
Sparse Core Ops, SparseCore 0:
  500.5 134.1 all-reduce.1
where the time goes:
time: 645 us; the launch traced here: 643 us
  waiting for transfers between devices  397 us (62%)
  matrix products  74.6 us (12%)
  local copies, waits for them, and re-layouts  65.7 us (10%)
  other arithmetic  45.3 us (7%)
  starting transfers between devices  44.7 us (7%)
  between operations  14 us (2%)
    ppermute x16, waiting for transfers between devices, from_behind(): lax.ppermute(x, axis, [(i, (i + by) % devices) for i in range(devices)])  177 us
    psum x1, waiting for transfers between devices, on_device(): lax.psum(jnp.sum(final_state.astype(jnp.float32), axis=0).astype(jnp.bflo...  134 us
    dot_general x40, matrix products, project(): jnp.einsum('mnd,de->mne', values, weight, preferred_element_type=jnp.floa...  60.9 us
    ppermute x16, waiting for transfers between devices, with_halo(): before = lax.ppermute(last, axis, up)  54.5 us
    ppermute x16, waiting for transfers between devices, with_halo(): after = lax.ppermute(first, axis, down)  30.4 us
    gather x8, local copies, waits for them, and re-layouts, update_nodes(): jnp.take(sender_terms, sender_rows.reshape(-1), axis=1)  21.5 us
    ppermute x16, starting transfers between devices, with_halo(): before = lax.ppermute(last, axis, up)  21.3 us
    ppermute x16, starting transfers between devices, from_behind(): lax.ppermute(x, axis, [(i, (i + by) % devices) for i in range(devices)])  16.9 us
  transfers between devices with their start and end apart: 49, of which 49 were waited for; matrix products, arithmetic and copies ran while one was open for 2% of the time, Pallas kernels for 0%

commit v1 on v0

v1 whole, which is shorter than its diff:
```python
import jax
import jax.numpy as jnp
from jax import lax
from jax.experimental import pallas as pl
from jax.experimental.pallas import tpu as pltpu
from jax.sharding import PartitionSpec as P

BLK = 128
EPSILON = 1e-05
CHUNKS = 2
LANES = 128
MESH = pl.DeviceIdType.MESH


def shifted(axis, by):
    devices = lax.axis_size(axis)
    return lax.rem(lax.axis_index(axis) + by + devices, devices)


def mm(a, b):
    return jnp.dot(a, b, preferred_element_type=jnp.float32)


def centred(w):
    w = w.astype(jnp.float32)
    return (w - jnp.mean(w, axis=-1, keepdims=True)).astype(jnp.bfloat16)


def twice_half_silu(u):
    return u + u * jnp.tanh(u)


def kernel(
    members, mats, bias, gain, blocks, shifts,
    final_ref, mean_ref,
    w, st_in, st_out, own, halo, spread, recv_term, node_term, hid, fin, acc, acc_in, mean_b,
    w_sem, init_send, st_sem, st_send, halo_sem, halo_send, fin_sem,
    acc_sem, acc_send, mean_sem, mean_send,
):
    sections = lax.axis_size("section")
    units = sections
    s = lax.axis_index("section")
    e = lax.axis_index("ens")
    width = members.shape[-1]
    rows = BLK // CHUNKS
    slots = 6
    last = sections - 1
    pieces = width // LANES

    def chunk(j):
        return pl.ds(j * rows, rows)

    loads = [pltpu.make_async_copy(mats.at[0, i], w.at[i], w_sem.at[i]) for i in range(6)]
    for i in (0, 1, 3, 2, 4, 5):
        loads[i].start()

    barrier = pltpu.get_barrier_semaphore()
    for by in range(1, sections):
        pl.semaphore_signal(barrier, inc=1, device_id={"section": shifted("section", by)}, device_id_type=MESH)
    for by in (1, -1):
        pl.semaphore_signal(barrier, inc=1, device_id={"dom": shifted("dom", by)}, device_id_type=MESH)
    pl.semaphore_signal(barrier, inc=1, device_id={"ens": 1 - e}, device_id_type=MESH)
    pl.semaphore_wait(barrier, sections + 2)

    def init_copy(j):
        return pltpu.make_async_remote_copy(
            members.at[0, chunk(j)], st_in.at[s, chunk(j)], init_send.at[j], st_sem.at[s, j],
            device_id={"section": 0}, device_id_type=MESH)

    def init_local(j):
        return pltpu.make_async_copy(members.at[0, chunk(j)], st_in.at[0, chunk(j)], st_sem.at[0, j])

    def state_copy(m, j):
        return pltpu.make_async_remote_copy(
            st_out.at[m, chunk(j)], st_in.at[m, chunk(j)], st_send.at[m, j], st_sem.at[m, j],
            device_id={"section": lax.rem(s + 1, sections)}, device_id_type=MESH)

    def final_copy(m, j):
        return pltpu.make_async_remote_copy(
            st_out.at[m, chunk(j)], fin.at[chunk(j)], st_send.at[m, j], fin_sem.at[j],
            device_id={"section": m}, device_id_type=MESH)

    def halo_copy(m, side, j):
        return pltpu.make_async_remote_copy(
            own.at[m, chunk(j)], halo.at[m, side, chunk(j)], halo_send.at[m, side, j], halo_sem.at[m, side, j],
            device_id={"dom": shifted("dom", 1 - 2 * side)}, device_id_type=MESH)

    @pl.when(s != 0)
    def _():
        for j in range(CHUNKS):
            init_copy(j).start()

    @pl.when(s == 0)
    def _():
        for j in range(CHUNKS):
            init_local(j).start()

    for i in (0, 1, 3):
        loads[i].wait()
        w[i] = w[i] * jnp.bfloat16(0.5)

    def put_spread(parity, block, j, values):
        values = values.astype(jnp.float32)
        for c in range(pieces):
            part = values[:, c * LANES:(c + 1) * LANES]
            spread[parity, block, c, pl.ds(j * rows, rows), :] = part
            spread[parity, block, c, pl.ds(BLK + j * rows, rows), :] = part

    def enter(m):
        parity = lax.rem(m, 2)
        for j in range(CHUNKS):
            pltpu.make_async_copy(st_in.at[m, chunk(j)], st_in.at[m, chunk(j)], st_sem.at[m, j]).wait()
            terms = mm(st_in[m, chunk(j)], w[0]).astype(jnp.bfloat16)
            own[m, chunk(j)] = terms
            for side in range(2):
                halo_copy(m, side, j).start()
            put_spread(parity, 1, j, terms)
        state = st_in[m]
        recv_term[parity] = mm(state, w[1]) + 0.5 * bias[0, 0:1]
        node_term[parity] = mm(state, w[3]) + 0.5 * bias[0, 1:2]

    def finish(m):
        parity = lax.rem(m, 2)
        for j in range(CHUNKS):
            for side in range(2):
                halo_copy(m, side, j).wait_recv()
                put_spread(parity, 2 * side, j, halo[m, side, chunk(j)])
        for j in range(CHUNKS):
            for k in range(slots):
                block = blocks[0, k]
                start = shifts[0, k] + j * rows
                for c in range(pieces):
                    lanes = slice(c * LANES, (c + 1) * LANES)
                    u = spread[parity, block, c, pl.ds(start, rows), :] + recv_term[parity, chunk(j), lanes]
                    hid[j, pl.ds(k * rows, rows), lanes] = twice_half_silu(u).astype(jnp.bfloat16)
            edge = mm(hid[j], w[2])
            total = None
            for k in range(slots):
                part = edge[k * rows:(k + 1) * rows]
                spread_of = jnp.mean(part * part, axis=-1, keepdims=True)
                part = part * lax.rsqrt(spread_of + EPSILON)
                total = part if total is None else total + part
            messages = (total * gain[0, 0:1]).astype(jnp.bfloat16)
            u = mm(messages, w[4]) + node_term[parity, chunk(j)]
            out = mm(twice_half_silu(u).astype(jnp.bfloat16), w[5])
            spread_of = jnp.mean(out * out, axis=-1, keepdims=True)
            state = st_in[m, chunk(j)].astype(jnp.float32)
            state = (state + out * lax.rsqrt(spread_of + EPSILON) * gain[0, 1:2]).astype(jnp.bfloat16)
            st_out[m, chunk(j)] = state

            @pl.when(s != last)
            def _():
                state_copy(m, j).start()

            @pl.when(s == last)
            def _():
                @pl.when(m != last)
                def _():
                    final_copy(m, j).start()

                @pl.when(m == 0)
                def _():
                    acc[chunk(j)] = st_out[m, chunk(j)].astype(jnp.float32)

                @pl.when(m != 0)
                def _():
                    acc[chunk(j)] = acc[chunk(j)] + st_out[m, chunk(j)].astype(jnp.float32)

    def step(t, carry):
        @pl.when(t < units)
        def _():
            enter(t)

        @pl.when(t == 0)
        def _():
            for i in (2, 5):
                loads[i].wait()
                w[i] = centred(w[i])
            loads[4].wait()
            w[4] = w[4] * jnp.bfloat16(0.5)

        @pl.when(t > 0)
        def _():
            finish(t - 1)

        return carry

    lax.fori_loop(0, units + 1, step, 0)

    half = BLK // 2
    mine = pl.ds(pl.multiple_of(e * half, half), half)
    theirs = pl.ds(pl.multiple_of((1 - e) * half, half), half)

    def mean_out(m, slot):
        return pltpu.make_async_remote_copy(
            mean_b.at[mine], mean_b.at[mine], mean_send.at[slot], mean_sem.at[0],
            device_id={"section": m}, device_id_type=MESH)

    mean_peer = pltpu.make_async_remote_copy(
        mean_b.at[mine], mean_b.at[mine], mean_send.at[sections - 1], mean_sem.at[1],
        device_id={"ens": 1 - e}, device_id_type=MESH)
    acc_peer = pltpu.make_async_remote_copy(
        acc.at[theirs], acc_in, acc_send, acc_sem,
        device_id={"ens": 1 - e}, device_id_type=MESH)
    order = sorted(range(1, sections), key=lambda d: -min(d, sections - d))

    @pl.when(s == last)
    def _():
        acc_peer.start()
        acc_peer.wait()
        mean_b[mine] = ((acc[mine] + acc_in[...]) * (1.0 / (2 * sections))).astype(jnp.bfloat16)
        for slot, d in enumerate(order):
            mean_out(lax.rem(s + d, sections), slot).start()
        mean_peer.start()
        final_ref[0] = st_out[last]
        for slot, d in enumerate(order):
            mean_out(lax.rem(s + d, sections), slot).wait_send()

    @pl.when(s != last)
    def _():
        for j in range(CHUNKS):
            pltpu.make_async_copy(fin.at[chunk(j)], fin.at[chunk(j)], fin_sem.at[j]).wait()
        final_ref[0] = fin[...]
        pltpu.make_async_copy(mean_b.at[mine], mean_b.at[mine], mean_sem.at[0]).wait()
        mean_peer.start()

    mean_peer.wait_send()

    def drain(m, carry):
        for j in range(CHUNKS):
            for side in range(2):
                halo_copy(m, side, j).wait_send()

            @pl.when(s != last)
            def _():
                state_copy(m, j).wait_send()

            @pl.when(jnp.logical_and(s == last, m != last))
            def _():
                final_copy(m, j).wait_send()
        return carry

    lax.fori_loop(0, units, drain, 0)

    @pl.when(s != 0)
    def _():
        for j in range(CHUNKS):
            init_copy(j).wait_send()

    pltpu.make_async_copy(mean_b.at[theirs], mean_b.at[theirs], mean_sem.at[1]).wait()
    mean_ref[...] = mean_b[...].astype(jnp.float32)


def on_device(members, layer_mats, biases, norm_gains, edge_blocks, edge_shift):
    sections = lax.axis_size("section")
    width = members.shape[-1]
    bf16, f32 = jnp.bfloat16, jnp.float32
    dma = pltpu.SemaphoreType.DMA
    vmem = pl.BlockSpec(memory_space=pltpu.VMEM)
    smem = pl.BlockSpec(memory_space=pltpu.SMEM)
    return pl.pallas_call(
        kernel,
        out_shape=(
            jax.ShapeDtypeStruct((1, BLK, width), bf16),
            jax.ShapeDtypeStruct((BLK, width), f32),
        ),
        in_specs=[vmem, pl.BlockSpec(memory_space=pl.ANY), vmem, vmem, smem, smem],
        out_specs=(vmem, vmem),
        scratch_shapes=[
            pltpu.VMEM((6, width, width), bf16),
            pltpu.VMEM((sections, BLK, width), bf16),
            pltpu.VMEM((sections, BLK, width), bf16),
            pltpu.VMEM((sections, BLK, width), bf16),
            pltpu.VMEM((sections, 2, BLK, width), bf16),
            pltpu.VMEM((2, 3, width // LANES, 2 * BLK, LANES), f32),
            pltpu.VMEM((2, BLK, width), f32),
            pltpu.VMEM((2, BLK, width), f32),
            pltpu.VMEM((CHUNKS, 6 * BLK // CHUNKS, width), bf16),
            pltpu.VMEM((BLK, width), bf16),
            pltpu.VMEM((BLK, width), f32),
            pltpu.VMEM((BLK // 2, width), f32),
            pltpu.VMEM((BLK, width), bf16),
            dma((6,)),
            dma((CHUNKS,)),
            dma((sections, CHUNKS)),
            dma((sections, CHUNKS)),
            dma((sections, 2, CHUNKS)),
            dma((sections, 2, CHUNKS)),
            dma((CHUNKS,)),
            dma,
            dma,
            dma((2,)),
            dma((sections,)),
        ],
        compiler_params=pltpu.CompilerParams(
            collective_id=0, has_side_effects=True, vmem_limit_bytes=48 << 20),
    )(members, layer_mats, biases, norm_gains, edge_blocks, edge_shift)


def solution(mesh):
    placed = (
        P(("section", "ens"), "dom", None),
        P("section", None, None, None),
        P("section", None, None),
        P("section", None, None),
        P("dom", None),
        P("dom", None),
    )
    return jax.shard_map(
        on_device,
        mesh=mesh,
        in_specs=placed,
        out_specs=(P(("section", "ens"), "dom", None), P("dom", None)),
        check_vma=False,
    )
```

time: 645 us -> 149 us (0.23)
  waiting for transfers between devices: 397 us -> 0 us
  Pallas kernels: 0 us -> 141 us
  matrix products: 74.6 us -> 0 us
  local copies, waits for them, and re-layouts: 65.7 us -> 6.83 us
  other arithmetic: 45.3 us -> 0 us
  starting transfers between devices: 44.7 us -> 0 us
  between operations: 14 us -> 0.65 us
    ppermute x48 -> x0, waiting for transfers between devices: 262 us -> none  [the longest x16 177 us: from_behind(): lax.ppermute(x, axis, [(i, (i + by) % devices) for i in range(devices)])]
    pallas_call x0 -> x1, Pallas kernels: none -> 141 us  [on_device(): pl.pallas_call(kernel, out_shape=(jax.ShapeDtypeStruct((1, BLK, width), b...]
    psum x1 -> x0, waiting for transfers between devices: 134 us -> none  [on_device(): lax.psum(jnp.sum(final_state.astype(jnp.float32), axis=0).astype(jnp.bflo...]
    dot_general x48 -> x0, matrix products: 74.6 us -> none  [the longest x40 60.9 us: project(): jnp.einsum('mnd,de->mne', values, weight, preferred_element_type=jnp.floa...]
    ppermute x48 -> x0, starting transfers between devices: 44.6 us -> none  [the longest x16 21.3 us: with_halo(): before = lax.ppermute(last, axis, up)]
    gather x8 -> x0, local copies, waits for them, and re-layouts: 21.5 us -> none  [update_nodes(): jnp.take(sender_terms, sender_rows.reshape(-1), axis=1)]
    convert_element_type x16 -> x0, other arithmetic: 17.8 us -> none  [the longest x8 13.6 us: update_nodes(): (state.astype(jnp.float32) + layer_norm(node_out) * gain_pair[1]).astype(...]
    add x16 -> x0, local copies, waits for them, and re-layouts: 13.1 us -> none  [update_nodes(): pre_act = picked.astype(jnp.float32) + receiver_terms[:, :, None, :]]
  transfers between devices with their start and end apart: 49 -> 0, of which waited for: 49 -> 0; matrix products, arithmetic and copies ran while one was open for 2% -> 0% of each run, Pallas kernels for 0% -> 0%
where the time goes in v1:
time: 149 us
  Pallas kernels  141 us (95%)
  local copies, waits for them, and re-layouts  6.83 us (5%)
    pallas_call x1, Pallas kernels, on_device(): pl.pallas_call(kernel, out_shape=(jax.ShapeDtypeStruct((1, BLK, width), b...  141 us
    unnamed x14, local copies, waits for them, and re-layouts  6.83 us

profile of v1, /device:TPU:1, one launch (start us, length us, event | category | flops | bytes accessed | tf_op | source)
XLA Modules:
  0.0 148.8 jit_solution(13575374199869725542)
XLA Ops:
  0.6 0.0 copy-start
  0.6 1.9 %copy-done = bf16[1,6,512,512]{3,2,1,0:T(8,128)(2,1)S(1)} copy-done((bf16[1,6,512,512]{3,2,1,0:T(8,128)(2,1)S(1)}, bf16[1,6,512,512]{3,2,1,0:T(8,128)(2,1)}, u32[]{:S(2)}) %copy-start) | copy-done | bytes 3145752
  2.5 0.0 copy-start.1
  2.5 0.9 copy-done.1
  3.4 0.0 copy-start.2
  3.4 0.7 copy-done.2
  4.1 0.0 copy-start.3
  4.1 0.7 copy-done.3
  4.8 0.0 copy-start.4
  4.8 0.7 copy-done.4
  5.5 0.0 copy-start.5
  5.5 0.7 copy-done.5
  6.1 141.3 %shard_map.77 = (bf16[1,128,512]{2,1,0:T(8,128)(2,1)S(1)}, f32[128,512]{1,0:T(8,128)S(1)}) custom-call(bf16[1,128,512]{2,1,0:T(8,128)(2,1)S(1)} %copy-done.1, bf16[1,6,512,512]{3,2,1,0:T(8,128)(2,1)S(1)} %copy-done, f32[1,2,512]{2,1,0:T(2,128)S(1)} %copy-done.2, f32[1,2,512]{2,1,0:T(2,128)S(1)} %copy-done.3, s32[1,6]{1,0:T(1,128)S(1)} %copy-done.4, ...), custom_call_target="tpu_custom_call" | custom-call | tf_op jit(solution)/shard_map/pallas_call | solution.py:261
  147.4 0.7 copy.10
  148.1 0.7 copy.11
Async XLA Ops:
  0.6 1.9 %copy-start = (bf16[1,6,512,512]{3,2,1,0:T(8,128)(2,1)S(1)}, bf16[1,6,512,512]{3,2,1,0:T(8,128)(2,1)}, u32[]{:S(2)}) copy-start(bf16[1,6,512,512]{3,2,1,0:T(8,128)(2,1)} %mats.1) | copy-start | bytes 9437188
  2.5 0.9 copy-start.1
  3.4 0.7 copy-start.2
  4.1 0.7 copy-start.3
  4.8 0.7 copy-start.4
  5.5 0.7 copy-start.5

commit v2 on v1

--- a/solution.py
+++ b/solution.py
@@ -7,7 +7,7 @@
 
 BLK = 128
 EPSILON = 1e-05
-CHUNKS = 2
+CHUNKS = 4
 LANES = 128
 MESH = pl.DeviceIdType.MESH
 
@@ -31,11 +31,11 @@
 
 
 def kernel(
-    members, mats, bias, gain, blocks, shifts,
+    members, mats, bias_in, gain_in, blocks_in, shifts_in,
     final_ref, mean_ref,
-    w, st_in, st_out, own, halo, spread, recv_term, node_term, hid, fin, acc, acc_in, mean_b,
-    w_sem, init_send, st_sem, st_send, halo_sem, halo_send, fin_sem,
-    acc_sem, acc_send, mean_sem, mean_send,
+    bias, gain, blocks, shifts, w, st_in, st_out, own, halo, spread, recv_term, node_term, hid, fin, acc, acc_in, mean_b, mean_f,
+    small_sem, w_sem, init_send, st_sem, st_send, halo_sem, halo_send, fin_sem,
+    acc_sem, acc_send, mean_sem, mean_send, out_sem, go_sem, turn_sem,
 ):
     sections = lax.axis_size("section")
     units = sections
@@ -51,8 +51,12 @@
         return pl.ds(j * rows, rows)
 
     loads = [pltpu.make_async_copy(mats.at[0, i], w.at[i], w_sem.at[i]) for i in range(6)]
-    for i in (0, 1, 3, 2, 4, 5):
-        loads[i].start()
+    small = [
+        pltpu.make_async_copy(a, b, small_sem.at[i])
+        for i, (a, b) in enumerate(((blocks_in, blocks), (shifts_in, shifts), (bias_in, bias), (gain_in, gain)))
+    ]
+    for copy in [loads[0]] + small + [loads[i] for i in (1, 3, 2, 4, 5)]:
+        copy.start()
 
     barrier = pltpu.get_barrier_semaphore()
     for by in range(1, sections):
@@ -85,16 +89,29 @@
             own.at[m, chunk(j)], halo.at[m, side, chunk(j)], halo_send.at[m, side, j], halo_sem.at[m, side, j],
             device_id={"dom": shifted("dom", 1 - 2 * side)}, device_id_type=MESH)
 
+    relay = sections // 2
+
+    @pl.when(jnp.logical_and(s > 1, s <= relay))
+    def _():
+        pl.semaphore_wait(go_sem, 1)
+
     @pl.when(s != 0)
     def _():
         for j in range(CHUNKS):
             init_copy(j).start()
 
+    @pl.when(jnp.logical_and(s > 0, s < relay))
+    def _():
+        init_copy(0).wait_send()
+        pl.semaphore_signal(go_sem, inc=1, device_id={"section": s + 1}, device_id_type=MESH)
+
     @pl.when(s == 0)
     def _():
         for j in range(CHUNKS):
             init_local(j).start()
 
+    for copy in small:
+        copy.wait()
     for i in (0, 1, 3):
         loads[i].wait()
         w[i] = w[i] * jnp.bfloat16(0.5)
@@ -125,29 +142,28 @@
             for side in range(2):
                 halo_copy(m, side, j).wait_recv()
                 put_spread(parity, 2 * side, j, halo[m, side, chunk(j)])
-        for j in range(CHUNKS):
-            for k in range(slots):
-                block = blocks[0, k]
-                start = shifts[0, k] + j * rows
-                for c in range(pieces):
-                    lanes = slice(c * LANES, (c + 1) * LANES)
-                    u = spread[parity, block, c, pl.ds(start, rows), :] + recv_term[parity, chunk(j), lanes]
-                    hid[j, pl.ds(k * rows, rows), lanes] = twice_half_silu(u).astype(jnp.bfloat16)
-            edge = mm(hid[j], w[2])
-            total = None
-            for k in range(slots):
-                part = edge[k * rows:(k + 1) * rows]
-                spread_of = jnp.mean(part * part, axis=-1, keepdims=True)
-                part = part * lax.rsqrt(spread_of + EPSILON)
-                total = part if total is None else total + part
-            messages = (total * gain[0, 0:1]).astype(jnp.bfloat16)
-            u = mm(messages, w[4]) + node_term[parity, chunk(j)]
-            out = mm(twice_half_silu(u).astype(jnp.bfloat16), w[5])
-            spread_of = jnp.mean(out * out, axis=-1, keepdims=True)
-            state = st_in[m, chunk(j)].astype(jnp.float32)
-            state = (state + out * lax.rsqrt(spread_of + EPSILON) * gain[0, 1:2]).astype(jnp.bfloat16)
-            st_out[m, chunk(j)] = state
-
+        for k in range(slots):
+            block = blocks[0, k]
+            for c in range(pieces):
+                lanes = slice(c * LANES, (c + 1) * LANES)
+                u = spread[parity, block, c, pl.ds(shifts[0, k], BLK), :] + recv_term[parity, :, lanes]
+                hid[pl.ds(k * BLK, BLK), lanes] = twice_half_silu(u).astype(jnp.bfloat16)
+        edge = mm(hid[...], w[2])
+        total = None
+        for k in range(slots):
+            part = edge[k * BLK:(k + 1) * BLK]
+            spread_of = jnp.mean(part * part, axis=-1, keepdims=True)
+            part = part * lax.rsqrt(spread_of + EPSILON)
+            total = part if total is None else total + part
+        messages = (total * gain[0, 0:1]).astype(jnp.bfloat16)
+        u = mm(messages, w[4]) + node_term[parity]
+        out = mm(twice_half_silu(u).astype(jnp.bfloat16), w[5])
+        spread_of = jnp.mean(out * out, axis=-1, keepdims=True)
+        state = st_in[m].astype(jnp.float32)
+        state = (state + out * lax.rsqrt(spread_of + EPSILON) * gain[0, 1:2]).astype(jnp.bfloat16)
+        st_out[m] = state
+
+        for j in range(CHUNKS):
             @pl.when(s != last)
             def _():
                 state_copy(m, j).start()
@@ -165,6 +181,10 @@
                 @pl.when(m != 0)
                 def _():
                     acc[chunk(j)] = acc[chunk(j)] + st_out[m, chunk(j)].astype(jnp.float32)
+
+    @pl.when(jnp.logical_and(s == 0, e == 1))
+    def _():
+        pl.semaphore_wait(turn_sem, 1)
 
     def step(t, carry):
         @pl.when(t < units)
@@ -179,6 +199,10 @@
             loads[4].wait()
             w[4] = w[4] * jnp.bfloat16(0.5)
 
+            @pl.when(jnp.logical_and(s == 0, e == 0))
+            def _():
+                pl.semaphore_signal(turn_sem, inc=1, device_id={"ens": 1 - e}, device_id_type=MESH)
+
         @pl.when(t > 0)
         def _():
             finish(t - 1)
@@ -212,7 +236,7 @@
         for slot, d in enumerate(order):
             mean_out(lax.rem(s + d, sections), slot).start()
         mean_peer.start()
-        final_ref[0] = st_out[last]
+        pltpu.make_async_copy(st_out.at[last], final_ref.at[0], out_sem.at[0]).start()
         for slot, d in enumerate(order):
             mean_out(lax.rem(s + d, sections), slot).wait_send()
 
@@ -220,7 +244,7 @@
     def _():
         for j in range(CHUNKS):
             pltpu.make_async_copy(fin.at[chunk(j)], fin.at[chunk(j)], fin_sem.at[j]).wait()
-        final_ref[0] = fin[...]
+        pltpu.make_async_copy(fin, final_ref.at[0], out_sem.at[0]).start()
         pltpu.make_async_copy(mean_b.at[mine], mean_b.at[mine], mean_sem.at[0]).wait()
         mean_peer.start()
 
@@ -244,11 +268,19 @@
 
     @pl.when(s != 0)
     def _():
-        for j in range(CHUNKS):
+        for j in range(1, CHUNKS):
             init_copy(j).wait_send()
 
+    @pl.when(s >= relay)
+    def _():
+        init_copy(0).wait_send()
+
     pltpu.make_async_copy(mean_b.at[theirs], mean_b.at[theirs], mean_sem.at[1]).wait()
-    mean_ref[...] = mean_b[...].astype(jnp.float32)
+    mean_f[...] = mean_b[...].astype(jnp.float32)
+    mean_done = pltpu.make_async_copy(mean_f, mean_ref, out_sem.at[1])
+    mean_done.start()
+    pltpu.make_async_copy(fin, final_ref.at[0], out_sem.at[0]).wait()
+    mean_done.wait()
 
 
 def on_device(members, layer_mats, biases, norm_gains, edge_blocks, edge_shift):
@@ -256,17 +288,20 @@
     width = members.shape[-1]
     bf16, f32 = jnp.bfloat16, jnp.float32
     dma = pltpu.SemaphoreType.DMA
-    vmem = pl.BlockSpec(memory_space=pltpu.VMEM)
-    smem = pl.BlockSpec(memory_space=pltpu.SMEM)
+    anywhere = pl.BlockSpec(memory_space=pl.ANY)
     return pl.pallas_call(
         kernel,
         out_shape=(
             jax.ShapeDtypeStruct((1, BLK, width), bf16),
             jax.ShapeDtypeStruct((BLK, width), f32),
         ),
-        in_specs=[vmem, pl.BlockSpec(memory_space=pl.ANY), vmem, vmem, smem, smem],
-        out_specs=(vmem, vmem),
+        in_specs=[anywhere] * 6,
+        out_specs=(anywhere, anywhere),
         scratch_shapes=[
+            pltpu.VMEM((1, 2, width), f32),
+            pltpu.VMEM((1, 2, width), f32),
+            pltpu.SMEM((1, 6), jnp.int32),
+            pltpu.SMEM((1, 6), jnp.int32),
             pltpu.VMEM((6, width, width), bf16),
             pltpu.VMEM((sections, BLK, width), bf16),
             pltpu.VMEM((sections, BLK, width), bf16),
@@ -275,11 +310,13 @@
             pltpu.VMEM((2, 3, width // LANES, 2 * BLK, LANES), f32),
             pltpu.VMEM((2, BLK, width), f32),
             pltpu.VMEM((2, BLK, width), f32),
-            pltpu.VMEM((CHUNKS, 6 * BLK // CHUNKS, width), bf16),
+            pltpu.VMEM((6 * BLK, width), bf16),
             pltpu.VMEM((BLK, width), bf16),
             pltpu.VMEM((BLK, width), f32),
             pltpu.VMEM((BLK // 2, width), f32),
             pltpu.VMEM((BLK, width), bf16),
+            pltpu.VMEM((BLK, width), f32),
+            dma((4,)),
             dma((6,)),
             dma((CHUNKS,)),
             dma((sections, CHUNKS)),
@@ -291,9 +328,12 @@
             dma,
             dma((2,)),
             dma((sections,)),
+            dma((2,)),
+            pltpu.SemaphoreType.REGULAR,
+            pltpu.SemaphoreType.REGULAR,
         ],
         compiler_params=pltpu.CompilerParams(
-            collective_id=0, has_side_effects=True, vmem_limit_bytes=48 << 20),
+            collective_id=0, has_side_effects=True, vmem_limit_bytes=60 << 20),
     )(members, layer_mats, biases, norm_gains, edge_blocks, edge_shift)
 
 

time: 149 us -> 138 us (0.926)
  Pallas kernels: 141 us -> 134 us
  local copies, waits for them, and re-layouts: 6.83 us -> 3.24 us
    pallas_call x1, Pallas kernels: 141 us -> 134 us  [on_device(): pl.pallas_call(kernel, out_shape=(jax.ShapeDtypeStruct((1, BLK, width), b...]
    unnamed x14 -> x2, local copies, waits for them, and re-layouts: 6.83 us -> 3.24 us
where the time goes in v2:
time: 138 us
  Pallas kernels  134 us (97%)
  local copies, waits for them, and re-layouts  3.24 us (2%)
    pallas_call x1, Pallas kernels, on_device(): pl.pallas_call(kernel, out_shape=(jax.ShapeDtypeStruct((1, BLK, width), b...  134 us
    unnamed x2, local copies, waits for them, and re-layouts  3.24 us

profile of v2, /device:TPU:1, one launch (start us, length us, event | category | flops | bytes accessed | tf_op | source)
XLA Modules:
  0.0 137.9 jit_solution(2523029424382458850)
XLA Ops:
  0.6 134.0 %shard_map.77 = (bf16[1,128,512]{2,1,0:T(8,128)(2,1)}, f32[128,512]{1,0:T(8,128)}) custom-call(bf16[1,128,512]{2,1,0:T(8,128)(2,1)} %members.1, bf16[1,6,512,512]{3,2,1,0:T(8,128)(2,1)} %mats.1, f32[1,2,512]{2,1,0:T(2,128)} %bias_in.1, f32[1,2,512]{2,1,0:T(2,128)} %gain_in.1, s32[1,6]{1,0:T(1,128)} %blocks_in.1, s32[1,6]{1,0:T(1,128)} %shifts_in.1), custom_call_target="tpu_custom_call" | custom-call | tf_op jit(solution)/shard_map/pallas_call | solution.py:292
  134.6 1.6 %copy.10 = bf16[1,128,512]{2,1,0:T(8,128)(2,1)} copy(bf16[1,128,512]{2,1,0:T(8,128)(2,1)} %get-tuple-element.4) | data formatting | bytes 262144
  136.2 1.7 %copy.11 = f32[128,512]{1,0:T(8,128)} copy(f32[128,512]{1,0:T(8,128)} %get-tuple-element.5) | data formatting | bytes 524288

commit v3 on v2

--- a/solution.py
+++ b/solution.py
@@ -47,6 +47,10 @@
     last = sections - 1
     pieces = width // LANES
 
+    d = lax.axis_index("dom")
+    after = (lax.rem(s + 1, sections), d, e)
+    beside = [(s, shifted("dom", by), e) for by in (1, -1)]
+
     def chunk(j):
         return pl.ds(j * rows, rows)
 
@@ -77,17 +81,17 @@
     def state_copy(m, j):
         return pltpu.make_async_remote_copy(
             st_out.at[m, chunk(j)], st_in.at[m, chunk(j)], st_send.at[m, j], st_sem.at[m, j],
-            device_id={"section": lax.rem(s + 1, sections)}, device_id_type=MESH)
+            device_id=after, device_id_type=MESH)
 
     def final_copy(m, j):
         return pltpu.make_async_remote_copy(
             st_out.at[m, chunk(j)], fin.at[chunk(j)], st_send.at[m, j], fin_sem.at[j],
-            device_id={"section": m}, device_id_type=MESH)
+            device_id=(m, d, e), device_id_type=MESH)
 
     def halo_copy(m, side, j):
         return pltpu.make_async_remote_copy(
-            own.at[m, chunk(j)], halo.at[m, side, chunk(j)], halo_send.at[m, side, j], halo_sem.at[m, side, j],
-            device_id={"dom": shifted("dom", 1 - 2 * side)}, device_id_type=MESH)
+            own.at[m, chunk(j)], halo.at[m, side, chunk(j)], halo_send.at[m], halo_sem.at[m],
+            device_id=beside[side], device_id_type=MESH)
 
     relay = sections // 2
 
@@ -138,9 +142,9 @@
 
     def finish(m):
         parity = lax.rem(m, 2)
+        pltpu.make_async_copy(halo.at[m], halo.at[m], halo_sem.at[m]).wait()
         for j in range(CHUNKS):
             for side in range(2):
-                halo_copy(m, side, j).wait_recv()
                 put_spread(parity, 2 * side, j, halo[m, side, chunk(j)])
         for k in range(slots):
             block = blocks[0, k]
@@ -163,24 +167,25 @@
         state = (state + out * lax.rsqrt(spread_of + EPSILON) * gain[0, 1:2]).astype(jnp.bfloat16)
         st_out[m] = state
 
-        for j in range(CHUNKS):
-            @pl.when(s != last)
-            def _():
+        @pl.when(s != last)
+        def _():
+            for j in range(CHUNKS):
                 state_copy(m, j).start()
 
-            @pl.when(s == last)
-            def _():
-                @pl.when(m != last)
-                def _():
+        @pl.when(s == last)
+        def _():
+            @pl.when(m != last)
+            def _():
+                for j in range(CHUNKS):
                     final_copy(m, j).start()
 
-                @pl.when(m == 0)
-                def _():
-                    acc[chunk(j)] = st_out[m, chunk(j)].astype(jnp.float32)
-
-                @pl.when(m != 0)
-                def _():
-                    acc[chunk(j)] = acc[chunk(j)] + st_out[m, chunk(j)].astype(jnp.float32)
+            @pl.when(m == 0)
+            def _():
+                acc[...] = st_out[m].astype(jnp.float32)
+
+            @pl.when(m != 0)
+            def _():
+                acc[...] = acc[...] + st_out[m].astype(jnp.float32)
 
     @pl.when(jnp.logical_and(s == 0, e == 1))
     def _():
@@ -251,10 +256,8 @@
     mean_peer.wait_send()
 
     def drain(m, carry):
-        for j in range(CHUNKS):
-            for side in range(2):
-                halo_copy(m, side, j).wait_send()
-
+        pltpu.make_async_copy(halo.at[m], halo.at[m], halo_send.at[m]).wait()
+        for j in range(CHUNKS):
             @pl.when(s != last)
             def _():
                 state_copy(m, j).wait_send()
@@ -321,8 +324,8 @@
             dma((CHUNKS,)),
             dma((sections, CHUNKS)),
             dma((sections, CHUNKS)),
-            dma((sections, 2, CHUNKS)),
-            dma((sections, 2, CHUNKS)),
+            dma((sections,)),
+            dma((sections,)),
             dma((CHUNKS,)),
             dma,
             dma,

time: 138 us -> 137 us (level)
  no operation moved by 1% of the time
where the time goes in v3:
time: 137 us
  Pallas kernels  133 us (97%)
  local copies, waits for them, and re-layouts  3.24 us (2%)
    pallas_call x1, Pallas kernels, on_device(): pl.pallas_call(kernel, out_shape=(jax.ShapeDtypeStruct((1, BLK, width), b...  133 us
    unnamed x2, local copies, waits for them, and re-layouts  3.24 us

profile of v3, /device:TPU:1, one launch (start us, length us, event | category | flops | bytes accessed | tf_op | source)
XLA Modules:
  0.0 137.2 jit_solution(13978188725312771323)
XLA Ops:
  0.6 133.3 %shard_map.77 = (bf16[1,128,512]{2,1,0:T(8,128)(2,1)}, f32[128,512]{1,0:T(8,128)}) custom-call(bf16[1,128,512]{2,1,0:T(8,128)(2,1)} %members.1, bf16[1,6,512,512]{3,2,1,0:T(8,128)(2,1)} %mats.1, f32[1,2,512]{2,1,0:T(2,128)} %bias_in.1, f32[1,2,512]{2,1,0:T(2,128)} %gain_in.1, s32[1,6]{1,0:T(1,128)} %blocks_in.1, s32[1,6]{1,0:T(1,128)} %shifts_in.1), custom_call_target="tpu_custom_call" | custom-call | tf_op jit(solution)/shard_map/pallas_call | solution.py:295
  134.0 1.6 %copy.10 = bf16[1,128,512]{2,1,0:T(8,128)(2,1)} copy(bf16[1,128,512]{2,1,0:T(8,128)(2,1)} %get-tuple-element.4) | data formatting | bytes 262144
  135.5 1.7 %copy.11 = f32[128,512]{1,0:T(8,128)} copy(f32[128,512]{1,0:T(8,128)} %get-tuple-element.5) | data formatting | bytes 524288

commit v4 on v3

--- a/solution.py
+++ b/solution.py
@@ -33,7 +33,7 @@
 def kernel(
     members, mats, bias_in, gain_in, blocks_in, shifts_in,
     final_ref, mean_ref,
-    bias, gain, blocks, shifts, w, st_in, st_out, own, halo, spread, recv_term, node_term, hid, fin, acc, acc_in, mean_b, mean_f,
+    bias, gain, blocks, shifts, w, st_in, st_out, own, halo, spread, recv_term, node_term, hid, fin, acc, acc_in, mean_b,
     small_sem, w_sem, init_send, st_sem, st_send, halo_sem, halo_send, fin_sem,
     acc_sem, acc_send, mean_sem, mean_send, out_sem, go_sem, turn_sem,
 ):
@@ -68,57 +68,57 @@
     for by in (1, -1):
         pl.semaphore_signal(barrier, inc=1, device_id={"dom": shifted("dom", by)}, device_id_type=MESH)
     pl.semaphore_signal(barrier, inc=1, device_id={"ens": 1 - e}, device_id_type=MESH)
-    pl.semaphore_wait(barrier, sections + 2)
-
-    def init_copy(j):
-        return pltpu.make_async_remote_copy(
-            members.at[0, chunk(j)], st_in.at[s, chunk(j)], init_send.at[j], st_sem.at[s, j],
-            device_id={"section": 0}, device_id_type=MESH)
-
-    def init_local(j):
-        return pltpu.make_async_copy(members.at[0, chunk(j)], st_in.at[0, chunk(j)], st_sem.at[0, j])
-
-    def state_copy(m, j):
-        return pltpu.make_async_remote_copy(
-            st_out.at[m, chunk(j)], st_in.at[m, chunk(j)], st_send.at[m, j], st_sem.at[m, j],
-            device_id=after, device_id_type=MESH)
-
-    def final_copy(m, j):
-        return pltpu.make_async_remote_copy(
-            st_out.at[m, chunk(j)], fin.at[chunk(j)], st_send.at[m, j], fin_sem.at[j],
-            device_id=(m, d, e), device_id_type=MESH)
-
-    def halo_copy(m, side, j):
-        return pltpu.make_async_remote_copy(
-            own.at[m, chunk(j)], halo.at[m, side, chunk(j)], halo_send.at[m], halo_sem.at[m],
-            device_id=beside[side], device_id_type=MESH)
-
-    relay = sections // 2
-
-    @pl.when(jnp.logical_and(s > 1, s <= relay))
-    def _():
-        pl.semaphore_wait(go_sem, 1)
-
-    @pl.when(s != 0)
-    def _():
-        for j in range(CHUNKS):
-            init_copy(j).start()
-
-    @pl.when(jnp.logical_and(s > 0, s < relay))
-    def _():
-        init_copy(0).wait_send()
-        pl.semaphore_signal(go_sem, inc=1, device_id={"section": s + 1}, device_id_type=MESH)
-
-    @pl.when(s == 0)
-    def _():
-        for j in range(CHUNKS):
-            init_local(j).start()
-
     for copy in small:
         copy.wait()
     for i in (0, 1, 3):
         loads[i].wait()
         w[i] = w[i] * jnp.bfloat16(0.5)
+    pl.semaphore_wait(barrier, sections + 2)
+
+    def init_copy(j):
+        return pltpu.make_async_remote_copy(
+            members.at[0, chunk(j)], st_in.at[s, chunk(j)], init_send.at[j], st_sem.at[s, j],
+            device_id={"section": 0}, device_id_type=MESH)
+
+    def init_local(j):
+        return pltpu.make_async_copy(members.at[0, chunk(j)], st_in.at[0, chunk(j)], st_sem.at[0, j])
+
+    def state_copy(m, j):
+        return pltpu.make_async_remote_copy(
+            st_out.at[m, chunk(j)], st_in.at[m, chunk(j)], st_send.at[m, j], st_sem.at[m, j],
+            device_id=after, device_id_type=MESH)
+
+    def final_copy(m, j):
+        return pltpu.make_async_remote_copy(
+            st_out.at[m, chunk(j)], fin.at[chunk(j)], st_send.at[m, j], fin_sem.at[j],
+            device_id=(m, d, e), device_id_type=MESH)
+
+    def halo_copy(m, side, j):
+        return pltpu.make_async_remote_copy(
+            own.at[m, chunk(j)], halo.at[m, side, chunk(j)], halo_send.at[m], halo_sem.at[m],
+            device_id=beside[side], device_id_type=MESH)
+
+    relay = sections // 2
+
+    @pl.when(jnp.logical_and(s > 1, s <= relay))
+    def _():
+        pl.semaphore_wait(go_sem, 1)
+
+    @pl.when(s != 0)
+    def _():
+        for j in range(CHUNKS):
+            init_copy(j).start()
+
+    @pl.when(jnp.logical_and(s > 0, s < relay))
+    def _():
+        init_copy(0).wait_send()
+        pl.semaphore_signal(go_sem, inc=1, device_id={"section": s + 1}, device_id_type=MESH)
+
+    @pl.when(s == 0)
+    def _():
+        for j in range(CHUNKS):
+            init_local(j).start()
+
 
     def put_spread(parity, block, j, values):
         values = values.astype(jnp.float32)
@@ -242,6 +242,32 @@
             mean_out(lax.rem(s + d, sections), slot).start()
         mean_peer.start()
         pltpu.make_async_copy(st_out.at[last], final_ref.at[0], out_sem.at[0]).start()
+
+    def drain(m, carry):
+        pltpu.make_async_copy(halo.at[m], halo.at[m], halo_send.at[m]).wait()
+        for j in range(CHUNKS):
+            @pl.when(s != last)
+            def _():
+                state_copy(m, j).wait_send()
+
+            @pl.when(jnp.logical_and(s == last, m != last))
+            def _():
+                final_copy(m, j).wait_send()
+        return carry
+
+    lax.fori_loop(0, units, drain, 0)
+
+    @pl.when(s != 0)
+    def _():
+        for j in range(1, CHUNKS):
+            init_copy(j).wait_send()
+
+    @pl.when(s >= relay)
+    def _():
+        init_copy(0).wait_send()
+
+    @pl.when(s == last)
+    def _():
         for slot, d in enumerate(order):
             mean_out(lax.rem(s + d, sections), slot).wait_send()
 
@@ -253,35 +279,10 @@
         pltpu.make_async_copy(mean_b.at[mine], mean_b.at[mine], mean_sem.at[0]).wait()
         mean_peer.start()
 
+    pltpu.make_async_copy(mean_b.at[theirs], mean_b.at[theirs], mean_sem.at[1]).wait()
+    mean_done = pltpu.make_async_copy(mean_b, mean_ref, out_sem.at[1])
+    mean_done.start()
     mean_peer.wait_send()
-
-    def drain(m, carry):
-        pltpu.make_async_copy(halo.at[m], halo.at[m], halo_send.at[m]).wait()
-        for j in range(CHUNKS):
-            @pl.when(s != last)
-            def _():
-                state_copy(m, j).wait_send()
-
-            @pl.when(jnp.logical_and(s == last, m != last))
-            def _():
-                final_copy(m, j).wait_send()
-        return carry
-
-    lax.fori_loop(0, units, drain, 0)
-
-    @pl.when(s != 0)
-    def _():
-        for j in range(1, CHUNKS):
-            init_copy(j).wait_send()
-
-    @pl.when(s >= relay)
-    def _():
-        init_copy(0).wait_send()
-
-    pltpu.make_async_copy(mean_b.at[theirs], mean_b.at[theirs], mean_sem.at[1]).wait()
-    mean_f[...] = mean_b[...].astype(jnp.float32)
-    mean_done = pltpu.make_async_copy(mean_f, mean_ref, out_sem.at[1])
-    mean_done.start()
     pltpu.make_async_copy(fin, final_ref.at[0], out_sem.at[0]).wait()
     mean_done.wait()
 
@@ -292,11 +293,11 @@
     bf16, f32 = jnp.bfloat16, jnp.float32
     dma = pltpu.SemaphoreType.DMA
     anywhere = pl.BlockSpec(memory_space=pl.ANY)
-    return pl.pallas_call(
+    final_state, mean = pl.pallas_call(
         kernel,
         out_shape=(
             jax.ShapeDtypeStruct((1, BLK, width), bf16),
-            jax.ShapeDtypeStruct((BLK, width), f32),
+            jax.ShapeDtypeStruct((BLK, width), bf16),
         ),
         in_specs=[anywhere] * 6,
         out_specs=(anywhere, anywhere),
@@ -318,7 +319,6 @@
             pltpu.VMEM((BLK, width), f32),
             pltpu.VMEM((BLK // 2, width), f32),
             pltpu.VMEM((BLK, width), bf16),
-            pltpu.VMEM((BLK, width), f32),
             dma((4,)),
             dma((6,)),
             dma((CHUNKS,)),
@@ -338,6 +338,7 @@
         compiler_params=pltpu.CompilerParams(
             collective_id=0, has_side_effects=True, vmem_limit_bytes=60 << 20),
     )(members, layer_mats, biases, norm_gains, edge_blocks, edge_shift)
+    return final_state, mean.astype(f32)
 
 
 def solution(mesh):

time: 137 us -> 137 us (level)
  local copies, waits for them, and re-layouts: 3.24 us -> 1.57 us
  other arithmetic: 0 us -> 1.63 us
    unnamed x2 -> x1, local copies, waits for them, and re-layouts: 3.24 us -> 1.57 us
    convert_element_type x0 -> x1, other arithmetic: none -> 1.63 us  [on_device(): return (final_state, mean.astype(f32))]
where the time goes in v4:
time: 137 us; the launch traced here: 136 us
  Pallas kernels  133 us (97%)
  other arithmetic  1.63 us (1%)
  local copies, waits for them, and re-layouts  1.57 us (1%)
    pallas_call x1, Pallas kernels, on_device(): pl.pallas_call(kernel, out_shape=(jax.ShapeDtypeStruct((1, BLK, width), b...  133 us

profile of v4, /device:TPU:1, one launch (start us, length us, event | category | flops | bytes accessed | tf_op | source)
XLA Modules:
  0.0 136.4 jit_solution(8949184064983600047)
XLA Ops:
  0.6 132.6 %shard_map.77 = (bf16[1,128,512]{2,1,0:T(8,128)(2,1)}, bf16[128,512]{1,0:T(8,128)(2,1)}) custom-call(bf16[1,128,512]{2,1,0:T(8,128)(2,1)} %members.1, bf16[1,6,512,512]{3,2,1,0:T(8,128)(2,1)} %mats.1, f32[1,2,512]{2,1,0:T(2,128)} %bias_in.1, f32[1,2,512]{2,1,0:T(2,128)} %gain_in.1, s32[1,6]{1,0:T(1,128)} %blocks_in.1, s32[1,6]{1,0:T(1,128)} %shifts_in.1), custom_call_target="tpu_custom_call" | custom-call | tf_op jit(solution)/shard_map/pallas_call | solution.py:296
  133.2 1.6 %convert_element_type.3 = f32[128,512]{1,0:T(8,128)} convert(bf16[128,512]{1,0:T(8,128)(2,1)} %get-tuple-element.5) | non-fusion elementwise | flops 65536 | bytes 393216 | tf_op jit(solution)/shard_map/convert_element_type | solution.py:341
  134.9 1.6 %copy.9 = bf16[1,128,512]{2,1,0:T(8,128)(2,1)} copy(bf16[1,128,512]{2,1,0:T(8,128)(2,1)} %get-tuple-element.8) | data formatting | bytes 262144

commit v5 on v4

--- a/solution.py
+++ b/solution.py
@@ -285,6 +285,19 @@
     mean_peer.wait_send()
     pltpu.make_async_copy(fin, final_ref.at[0], out_sem.at[0]).wait()
     mean_done.wait()
+
+
+def hand_out(state_in, mean_in, state_out, mean_out, narrow, wide, sems):
+    state = pltpu.make_async_copy(state_in, state_out, sems.at[0])
+    taken = pltpu.make_async_copy(mean_in, narrow, sems.at[1])
+    given = pltpu.make_async_copy(wide, mean_out, sems.at[2])
+    taken.start()
+    state.start()
+    taken.wait()
+    wide[...] = narrow[...].astype(jnp.float32)
+    given.start()
+    state.wait()
+    given.wait()
 
 
 def on_device(members, layer_mats, biases, norm_gains, edge_blocks, edge_shift):
@@ -338,7 +351,21 @@
         compiler_params=pltpu.CompilerParams(
             collective_id=0, has_side_effects=True, vmem_limit_bytes=60 << 20),
     )(members, layer_mats, biases, norm_gains, edge_blocks, edge_shift)
-    return final_state, mean.astype(f32)
+    return pl.pallas_call(
+        hand_out,
+        out_shape=(
+            jax.ShapeDtypeStruct((1, BLK, width), bf16),
+            jax.ShapeDtypeStruct((BLK, width), f32),
+        ),
+        in_specs=[anywhere] * 2,
+        out_specs=(anywhere, anywhere),
+        scratch_shapes=[
+            pltpu.VMEM((BLK, width), bf16),
+            pltpu.VMEM((BLK, width), f32),
+            dma((3,)),
+        ],
+        compiler_params=pltpu.CompilerParams(vmem_limit_bytes=60 << 20),
+    )(final_state, mean)
 
 
 def solution(mesh):

time: 137 us -> 139 us (1.015)
  Pallas kernels: 133 us -> 138 us
  other arithmetic: 1.63 us -> 0 us
  local copies, waits for them, and re-layouts: 1.57 us -> 0 us
    pallas_call x0 -> x1, Pallas kernels: none -> 5.1 us  [on_device(): pl.pallas_call(hand_out, out_shape=(jax.ShapeDtypeStruct((1, BLK, width),...]
    convert_element_type x1 -> x0, other arithmetic: 1.63 us -> none  [on_device(): return (final_state, mean.astype(f32))]
    unnamed x1 -> x0, local copies, waits for them, and re-layouts: 1.57 us -> none
where the time goes in v5:
time: 139 us; the launch traced here: 138 us
  Pallas kernels  138 us (99%)
    pallas_call x1, Pallas kernels, on_device(): pl.pallas_call(kernel, out_shape=(jax.ShapeDtypeStruct((1, BLK, width), b...  133 us
    pallas_call x1, Pallas kernels, on_device(): pl.pallas_call(hand_out, out_shape=(jax.ShapeDtypeStruct((1, BLK, width),...  5.1 us

profile of v5, /device:TPU:1, one launch (start us, length us, event | category | flops | bytes accessed | tf_op | source)
XLA Modules:
  0.0 138.4 jit_solution(3344799063121551650)
XLA Ops:
  0.6 132.6 %shard_map.77 = (bf16[1,128,512]{2,1,0:T(8,128)(2,1)}, bf16[128,512]{1,0:T(8,128)(2,1)}) custom-call(bf16[1,128,512]{2,1,0:T(8,128)(2,1)} %members.1, bf16[1,6,512,512]{3,2,1,0:T(8,128)(2,1)} %mats.1, f32[1,2,512]{2,1,0:T(2,128)} %bias_in.1, f32[1,2,512]{2,1,0:T(2,128)} %gain_in.1, s32[1,6]{1,0:T(1,128)} %blocks_in.1, s32[1,6]{1,0:T(1,128)} %shifts_in.1), custom_call_target="tpu_custom_call" | custom-call | tf_op jit(solution)/shard_map/pallas_call | solution.py:309
  133.2 5.1 %shard_map.78 = (bf16[1,128,512]{2,1,0:T(8,128)(2,1)}, f32[128,512]{1,0:T(8,128)}) custom-call(bf16[1,128,512]{2,1,0:T(8,128)(2,1)} %get-tuple-element.4.state_in, bf16[128,512]{1,0:T(8,128)(2,1)} %get-tuple-element.5.mean_in), custom_call_target="tpu_custom_call" | custom-call | tf_op jit(solution)/shard_map/pallas_call | solution.py:354
